TPU v7x, 128 devices: a whole 4x4x4 slice. The times are simulated.
128 devices in a mesh: subj: 16 (over y, z_lo, core), slab: 8 (over z_hi, x).
Axes of the slice: x: 4, y: 4, z: 4 (z_hi: 2, z_lo: 2; z = z_hi * 2 + z_lo), core: 2. Of those that a mesh axis runs over, the one named last changes fastest.
Arguments:
- template: float32 [8, 4096, 128], P('slab', 'subj'), may hold values from -6 to 6
- subject: bfloat16 [16, 8, 256, 128], P('subj', 'slab'), may hold values from -6 to 6
- tile_lists: int32 [16, 8, 4, 256], P('subj', 'slab'), may hold values from 0 to 4105, as said below
- corners: int32 [16, 8, 256, 8, 128], P('subj', 'slab'), may hold values from 0 to 511, as said below
- fractions: float32 [16, 8, 256, 3, 128], P('subj', 'slab'), may hold values from 0 to 1
- live_tiles: int32 [16, 8], P('subj', 'slab'), may hold values from 32 to 256, as said below
Outputs:
- new_atlas: float32 [8, 4096, 128], P('slab', 'subj')
- correlation: float32 [16, 8, 256], P('subj', 'slab')
Inputs may be any that keep to these rules, and one draw needn't show every extreme that they name: `tile_lists`: warped tile t lists base, base + 1, base + 8, base + 9 for one base from 0 to 4096; in every subject and slab warped tile 0 has base 0 and warped tile 1 has base 4096. The eight corners of a voxel are start + 0, 1, 4, 5, 16, 17, 20, 21 for one start a voxel, corner q adding 1, 4 and 16 for its bits 0, 1 and 2, so they are distinct. `live_tiles`: each entry is 256, 128, 64 or 32.
All inputs are finite; a program needn't handle non-finite values.
Results may differ from a plain program's by a relative error of at most 0.0014.
Values may be sent and summed in bfloat16 or wider, within the bound.
No kernel may reach another device: no remote copies, remote signals or barrier semaphores. Data moves between devices by JAX's collectives and lax.ppermute only.
A program may use at most 128 MiB of HBM per device.

v0:
```python
import jax
import jax.numpy as jnp
from jax import lax
from jax.experimental import pallas as pl
from jax.experimental.pallas import tpu as pltpu
from jax.sharding import PartitionSpec as P

TILE = 128
SLOTS = 4
ROW = 8
ITERS = 2
HALO = 5
RIM = 8
CAP = 36
PAD = 40
META = 3 * CAP
BLOCK = 3 * CAP + 4
COUNT_AT = 126
MOST_AT = 127
FRAC_UNIT = 65535.0
U_UNIT = float(2**27)
STEP = 64
PART = 64
GROUP = 32

epsilon = 1e-05
ascent = 40.0

SPOTS = (0, 1, ROW, ROW + 1)
SHIFTS = (0, 1, 4, 5)


def pieces_of(word):
    return [
        ((word >> shift) & 255).astype(jnp.float32).astype(jnp.bfloat16) for shift in (0, 8, 16, 24)
    ]


def pack_kernel(own_rows, live_ref, round_ref, lists_ref, corners_ref, fractions_ref, subject_ref, send_ref, slot_ref):
    groups = send_ref.shape[0] // BLOCK
    tiles = subject_ref.shape[0]
    base = lists_ref[0:1, :]
    alive = lax.broadcasted_iota(jnp.int32, (1, tiles), 1) < live_ref[0, 0]
    owner = jnp.minimum(base // own_rows, groups - 1)
    local = base - owner * own_rows
    group_iota = lax.broadcasted_iota(jnp.int32, (groups, tiles), 0)
    member = jnp.where((group_iota == owner) & alive, 1.0, 0.0)
    before = lax.broadcasted_iota(jnp.int32, (tiles, tiles), 0) < lax.broadcasted_iota(
        jnp.int32, (tiles, tiles), 1
    )
    earlier = jnp.dot(
        member.astype(jnp.bfloat16),
        jnp.where(before, 1.0, 0.0).astype(jnp.bfloat16),
        preferred_element_type=jnp.float32,
    )
    counts = jnp.sum(member, axis=1, keepdims=True)
    first = round_ref[0, 0] * CAP
    rank = jnp.sum(member * earlier, axis=0, keepdims=True).astype(jnp.int32) - first
    chosen = alive & (rank >= 0) & (rank < CAP)
    slot = jnp.where(chosen, owner * PAD + rank, -1)
    slot_ref[...] = slot
    pick = jnp.where(
        lax.broadcasted_iota(jnp.int32, (groups * PAD, tiles), 0) == slot, 1.0, 0.0
    ).astype(jnp.bfloat16)

    at_rank = jnp.where(
        (lax.broadcasted_iota(jnp.int32, (TILE, tiles), 0) == rank) & chosen, 1.0, 0.0
    ).astype(jnp.bfloat16)
    local_high = (member * (local >> 4).astype(jnp.float32)).astype(jnp.bfloat16)
    local_low = (member * (local & 15).astype(jnp.float32)).astype(jnp.bfloat16)
    across = (((1,), (1,)), ((), ()))
    bases = 16.0 * lax.dot_general(
        local_high, at_rank, across, preferred_element_type=jnp.float32
    ) + lax.dot_general(local_low, at_rank, across, preferred_element_type=jnp.float32)
    here = jnp.clip(counts.astype(jnp.int32) - first, 0, CAP)
    most = jnp.max(counts, axis=0, keepdims=True).astype(jnp.int32)
    lane = lax.broadcasted_iota(jnp.int32, (groups, TILE), 1)
    header = jnp.where(
        lane == COUNT_AT, here, jnp.where(lane == MOST_AT, most, bases.astype(jnp.int32))
    )

    target = subject_ref[...].astype(jnp.float32)
    centered = target - jnp.mean(target, axis=-1, keepdims=True)
    subject_var = jnp.mean(centered * centered, axis=-1, keepdims=True) + epsilon
    unit = centered / jnp.sqrt(subject_var)
    coded = [
        (fractions_ref[d] * FRAC_UNIT + 0.5).astype(jnp.int32) for d in range(3)
    ]
    words = (
        coded[0] | (coded[1] << 16),
        coded[2] | (corners_ref[:, 0, :] << 16),
        jnp.round(unit * U_UNIT).astype(jnp.int32),
    )
    for w, word in enumerate(words):
        data = jnp.concatenate(pieces_of(word), axis=1)
        moved = jnp.dot(pick, data, preferred_element_type=jnp.float32)
        low = (moved[:, :TILE] + 256.0 * moved[:, TILE : 2 * TILE]).astype(jnp.int32)
        high = (moved[:, 2 * TILE : 3 * TILE] + 256.0 * moved[:, 3 * TILE :]).astype(jnp.int32)
        whole = low | (high << 16)
        for g in range(groups):
            send_ref[pl.ds(g * BLOCK + w * CAP, CAP), :] = whole[g * PAD : g * PAD + CAP]
    for g in range(groups):
        send_ref[pl.ds(g * BLOCK + META, 4), :] = jnp.broadcast_to(header[g : g + 1], (4, TILE))


def compact(meta_ref, groups, base_of, from_row, slot_of):
    def source(s, state):
        def take(r, place):
            base_of[place] = meta_ref[s, r] + (RIM - HALO)
            from_row[place] = s * BLOCK + r
            slot_of[place] = s * PAD + r
            return place + 1

        place = lax.fori_loop(0, meta_ref[s, COUNT_AT], take, state[0])
        return place, jnp.maximum(state[1], meta_ref[s, MOST_AT])

    total, most = lax.fori_loop(0, groups, source, (jnp.int32(0), jnp.int32(0)))
    for extra in range(GROUP):
        base_of[total + extra] = 0
        from_row[total + extra] = 0
        slot_of[total + extra] = PAD - 1
    return total, (most + (CAP - 1)) // CAP


def fetch(total, recv_ref, from_row, words, table, base_of, foot):
    def body(step, carry):
        at = pl.multiple_of(step * 8, 8)
        for i in range(8):
            here = pl.ds(at + i, 1)
            if recv_ref is not None:
                row = from_row[at + i]
                for w in range(3):
                    words[w, here, :] = recv_ref[pl.ds(row + w * CAP, 1), :]
            base = base_of[at + i]
            for k, shift in enumerate(SPOTS):
                foot[k, here, :] = table[pl.ds(base + shift, 1), :]
        return carry

    lax.fori_loop(0, (total + 7) // 8, body, 0)


def fractions_of(first, second):
    return (
        (first & 65535).astype(jnp.float32) * (1.0 / FRAC_UNIT),
        lax.shift_right_logical(first, 16).astype(jnp.float32) * (1.0 / FRAC_UNIT),
        (second & 65535).astype(jnp.float32) * (1.0 / FRAC_UNIT),
    )


def weights_of(along):
    away = [1.0 - x for x in along]
    found = []
    for q in range(8):
        weight = (
            (along[0] if q & 1 else away[0])
            * (along[1] if q & 2 else away[1])
            * (along[2] if q & 4 else away[2])
        )
        found.append(weight.astype(jnp.bfloat16).astype(jnp.float32))
    return found


def sample(total, words, foot, give):
    def piece(at):
        here = pl.ds(at, PART)
        second = words[1, here, :]
        unit = words[2, here, :].astype(jnp.float32) * (1.0 / U_UNIT)
        start = lax.shift_right_logical(second, 16)
        tables = [foot[k, here, :] for k in range(SLOTS)]
        weights = weights_of(fractions_of(words[0, here, :], second))
        peak = jnp.abs(tables[0])
        for t in tables[1:]:
            peak = jnp.maximum(peak, jnp.abs(t))
        peak = jnp.max(peak, axis=-1, keepdims=True)
        scale = jnp.where(peak > 0.0, 32767.0 / peak, 0.0)
        codes = [jnp.round(t * scale).astype(jnp.int32) for t in tables]
        couples = [(codes[k] & 65535) | (codes[k + 1] << 16) for k in (0, 2)]
        warped = None
        for q in range(8):
            column = start + (SHIFTS[q & 3] + (16 if q & 4 else 0))
            lane = column & (TILE - 1)
            got = [
                jnp.take_along_axis(c, lane, axis=1, mode="promise_in_bounds", wrap_negative_indices=False)
                for c in couples
            ]
            word = jnp.where(column < 2 * TILE, got[0], got[1])
            word = lax.shift_left(word, 16 - ((column >> 3) & 16))
            picked = lax.shift_right_arithmetic(word, jnp.full_like(word, 16)).astype(jnp.float32)
            term = weights[q] * picked
            warped = term if warped is None else warped + term
        warped = warped * (peak * (1.0 / 32767.0))
        deviation = warped - jnp.mean(warped, axis=-1, keepdims=True)
        warp_var = jnp.mean(deviation * deviation, axis=-1, keepdims=True) + epsilon
        inverse = 1.0 / jnp.sqrt(warp_var)
        correl = jnp.mean(deviation * unit, axis=-1, keepdims=True) * inverse
        slope = (unit * inverse - (correl / warp_var) * deviation) * (1.0 / TILE)
        alive = at + lax.broadcasted_iota(jnp.int32, (PART, TILE), 0) < total
        slope = jnp.where(alive, slope, 0.0).astype(jnp.bfloat16).astype(jnp.float32)
        give(here, weights, start, slope, jnp.broadcast_to(correl, (PART, TILE)))

    def body(step, carry):
        for inner in range(0, STEP, PART):
            piece(pl.multiple_of(step * STEP + inner, PART))
        return carry

    lax.fori_loop(0, (total + (STEP - 1)) // STEP, body, 0)


def send_back(total, rows, slot_of, correl_ref):
    def body(step, carry):
        at = pl.multiple_of(step * 8, 8)
        for i in range(8):
            correl_ref[pl.ds(slot_of[at + i], 1), :] = rows[pl.ds(at + i, 1), :]
        return carry

    lax.fori_loop(0, (total + 7) // 8, body, 0)


def splat_all(total, starts, values, base_of, acc):
    acc[...] = jnp.zeros(acc.shape, jnp.float32)
    high_iota = lax.broadcasted_iota(jnp.int32, (32, TILE), 0)
    low_iota = lax.broadcasted_iota(jnp.int32, (16, TILE), 0)
    across = (((1,), (1,)), ((), ()))

    def body(step, carry):
        at = pl.multiple_of(step * GROUP, GROUP)
        for i in range(GROUP):
            line = pl.ds(at + i, 1)
            start = starts[line, :]
            high = (high_iota - (start >> 4)).astype(jnp.int16)
            low = (low_iota - (start & 15)).astype(jnp.int16)
            nothing = jnp.zeros((32, TILE), jnp.bfloat16)
            slope = jnp.broadcast_to(values[8, line, :], (32, TILE)).astype(jnp.bfloat16)
            sides = [jnp.where(high == jnp.int16(j), slope, nothing) for j in range(3)]
            corner = [
                jnp.broadcast_to(values[q, line, :], (16, TILE)).astype(jnp.bfloat16) for q in range(8)
            ]
            near, far = corner[:4], corner[4:]
            inside = [low == jnp.int16(shift) for shift in SHIFTS]
            wrapped = [low == jnp.int16(shift - 16) for shift in SHIFTS]
            parts = [nothing[:16] for _ in range(3)]
            for q in range(4):
                parts[0] = jnp.where(inside[q], near[q], parts[0])
                parts[1] = jnp.where(inside[q], far[q], parts[1])
                if q > 0:
                    parts[1] = jnp.where(wrapped[q], near[q], parts[1])
                    parts[2] = jnp.where(wrapped[q], far[q], parts[2])
            splat = lax.dot_general(
                jnp.concatenate(sides, axis=1),
                jnp.concatenate(parts, axis=1),
                across,
                preferred_element_type=jnp.float32,
            )
            base = base_of[at + i]
            spots = [pl.ds(pl.multiple_of((base + shift) * 8, 8), 8) for shift in SPOTS]
            sums = [acc[spots[k], 0:16] + splat[8 * k : 8 * k + 8] for k in range(SLOTS)]
            for k in range(SLOTS):
                acc[spots[k], 0:16] = sums[k]
        return carry

    lax.fori_loop(0, (total + (GROUP - 1)) // GROUP, body, 0)


def unfold(acc, rows):
    total = None
    for j in range(8):
        line = acc[pl.ds(j, rows, stride=8), :]
        line = pltpu.roll(line, 16 * j, 1) if j else line
        total = line if total is None else total + line
    return total


def fill_table(table, below, owned, above):
    count = owned.shape[0]
    for at, value in ((0, below), (RIM, owned), (RIM + count, above)):
        table[pl.ds(at, value.shape[0]), :] = value.astype(jnp.bfloat16).astype(jnp.float32)


def ascend_kernel(
    back, meta_ref, inside_ref, recv_ref, owned_ref, first_ref, second_ref,
    grad_ref, one_ref, two_ref, rounds_ref, total_ref, words, base_of, slot_of, correl_ref,
    table, foot, starts, values, acc, from_row,
):
    groups = recv_ref.shape[0] // BLOCK
    rows = grad_ref.shape[0]
    odd = inside_ref[0, 2] > 0.0
    one, two = first_ref[...], second_ref[...]
    fill_table(table, jnp.where(odd, two, one), owned_ref[...], jnp.where(odd, one, two))
    total, rounds = compact(meta_ref, groups, base_of, from_row, slot_of)
    rounds_ref[0, 0] = rounds
    total_ref[0, 0] = total
    fetch(total, recv_ref, from_row, words, table, base_of, foot)

    def give(here, weights, start, slope, correl):
        starts[here, :] = start
        for q in range(8):
            values[q, here, :] = weights[q]
        values[8, here, :] = slope
        if back:
            values[9, here, :] = correl

    sample(total, words, foot, give)
    if back:
        send_back(total, values.at[9], slot_of, correl_ref)
    splat_all(total, starts, values, base_of, acc)
    grad = unfold(acc, rows)
    grad_ref[...] = grad
    low, high = grad[: 2 * RIM], grad[rows - 2 * RIM :]
    one_ref[...] = jnp.where(odd, high, low)
    two_ref[...] = jnp.where(odd, low, high)


def forward_kernel(
    total_ref, base_of, slot_of, inside_ref, words, owned_ref, first_ref, second_ref, grad_ref, one_ref, two_ref,
    atlas_ref, slope_ref, correl_ref,
    table, foot, marks,
):
    own_rows = owned_ref.shape[0]
    rows = own_rows + 2 * RIM
    total = total_ref[0, 0]
    odd = inside_ref[0, 2] > 0.0
    one, two = one_ref[...], two_ref[...]
    first = grad_ref[0 : 2 * RIM, :] + jnp.where(odd, two, one)
    last = grad_ref[rows - 2 * RIM : rows, :] + jnp.where(odd, one, two)
    one, two = first_ref[...], second_ref[...]
    below = (jnp.where(odd, two, one) + ascent * first[:RIM]) * inside_ref[0, 0]
    above = (jnp.where(odd, one, two) + ascent * last[RIM:]) * inside_ref[0, 1]
    atlas_ref[0:RIM, :] = owned_ref[0:RIM, :] + ascent * first[RIM:]
    atlas_ref[RIM : own_rows - RIM, :] = (
        owned_ref[RIM : own_rows - RIM, :] + ascent * grad_ref[2 * RIM : own_rows, :]
    )
    atlas_ref[own_rows - RIM : own_rows, :] = owned_ref[own_rows - RIM : own_rows, :] + ascent * last[:RIM]
    fill_table(table, below, atlas_ref[...], above)
    fetch(total, None, None, None, table, base_of, foot)

    def give(here, weights, start, slope, correl):
        slope_ref[here, :] = slope
        marks[here, :] = correl

    sample(total, words, foot, give)
    send_back(total, marks, slot_of, correl_ref)


def backward_kernel(
    total_ref, base_of, inside_ref, words, slope_ref, atlas_ref, extra_ref,
    near_ref, one_ref, two_ref,
    starts, values, acc,
):
    own_rows = atlas_ref.shape[0]
    rows = own_rows + 2 * RIM
    total = total_ref[0, 0]

    def spread(step, carry):
        here = pl.ds(pl.multiple_of(step * STEP, STEP), STEP)
        second = words[1, here, :]
        values[8, here, :] = slope_ref[here, :]
        starts[here, :] = lax.shift_right_logical(second, 16)
        for q, weight in enumerate(weights_of(fractions_of(words[0, here, :], second))):
            values[q, here, :] = weight
        return carry

    lax.fori_loop(0, (total + (STEP - 1)) // STEP, spread, 0)
    splat_all(total, starts, values, base_of, acc)
    grad = unfold(acc, rows) + extra_ref[...]
    odd = inside_ref[0, 2] > 0.0
    low, high = grad[:RIM], grad[rows - RIM :]
    one_ref[...] = jnp.where(odd, high, low)
    two_ref[...] = jnp.where(odd, low, high)
    near_ref[...] = atlas_ref[...] + ascent * grad[RIM : RIM + own_rows]


def unpack_kernel(slot_ref, back_ref, extra_ref, correl_ref):
    slot = slot_ref[...]
    tiles = slot.shape[1]
    total = jnp.zeros((PAD, tiles), jnp.float32)
    inner = lax.broadcasted_iota(jnp.int32, (PAD, tiles), 0)
    for g in range(back_ref.shape[0] // PAD):
        block = back_ref[pl.ds(g * PAD, PAD), :]
        wide = jnp.concatenate([block] * (tiles // TILE), axis=1)
        total = total + jnp.where(inner == slot - g * PAD, wide, 0.0)
    correl_ref[...] = jnp.sum(total, axis=0, keepdims=True) + extra_ref[...]


def finish_kernel(
    inside_ref, near_ref, one_ref, two_ref, slot_ref, back_ref, extra_ref, atlas_ref, correl_ref
):
    odd = inside_ref[0, 2] > 0.0
    one, two = one_ref[...], two_ref[...]
    atlas_ref[...] = near_ref[...]
    atlas_ref[0:RIM, :] += ascent * jnp.where(odd, two, one)
    rows = atlas_ref.shape[0]
    atlas_ref[rows - RIM : rows, :] += ascent * jnp.where(odd, one, two)
    unpack_kernel(slot_ref, back_ref, extra_ref, correl_ref)


VMEM = pl.BlockSpec(memory_space=pltpu.VMEM)
SMEM = pl.BlockSpec(memory_space=pltpu.SMEM)
LIMIT = pltpu.CompilerParams(vmem_limit_bytes=48 * 1024 * 1024)


def shards(template, subject, tile_lists, corners, fractions, live_tiles):
    groups = lax.axis_size("subj")
    slabs = lax.axis_size("slab")
    owned = template[0]
    own_rows = owned.shape[0]
    tiles = subject.shape[2]
    rows = own_rows + 2 * RIM
    room = (groups * CAP + STEP) // STEP * STEP
    planes = jnp.transpose(fractions[0, 0], (1, 0, 2))
    f32, i32 = jnp.float32, jnp.int32

    def call(kernel, name, inputs, outputs, scratch=(), cost=3_000_000):
        return pl.pallas_call(
            kernel,
            out_shape=[jax.ShapeDtypeStruct(shape, kind) for shape, kind, _ in outputs],
            in_specs=[space for _, space in inputs],
            out_specs=[space for _, _, space in outputs],
            scratch_shapes=list(scratch),
            compiler_params=LIMIT,
            cost_estimate=pl.CostEstimate(flops=0, bytes_accessed=cost, transcendentals=0),
            name=name,
        )(*[value for value, _ in inputs])

    count = groups * slabs
    order = [(k % groups) * slabs + k // groups for k in range(count)]
    both = ("subj", "slab")
    place = lax.axis_index("slab") * groups + lax.axis_index("subj")
    odd = place % 2 == 1
    inside = jnp.stack([place > 0, place < count - 1, odd]).astype(f32).reshape(1, 3)

    def pairs_from(start):
        found = [(order[k], order[k + 1]) for k in range(start, count - 1, 2)]
        return found + [(there, here) for here, there in found]

    def swap(one, two):
        return lax.ppermute(one, both, pairs_from(1)), lax.ppermute(two, both, pairs_from(0))

    def sides(one, two):
        return jnp.where(odd, two, one), jnp.where(odd, one, two)

    def pack(number):
        def kernel(*refs):
            pack_kernel(own_rows, *refs)

        return call(
            kernel,
            "pack",
            [(live_tiles, SMEM), (number, SMEM), (tile_lists[0, 0], VMEM), (corners[0, 0], VMEM), (planes, VMEM), (subject[0, 0], VMEM)],
            [((groups * BLOCK, TILE), i32, VMEM), ((1, tiles), i32, VMEM)],
        )

    def exchange(send):
        return lax.all_to_all(send, "subj", 0, 0, tiled=True)

    def ascend(recv, one, owned, two, back):
        meta = recv.reshape(groups, BLOCK, TILE)[:, META, :]

        def kernel(*refs):
            ascend_kernel(back, *refs)

        return call(
            kernel,
            "ascend",
            [(meta, SMEM), (inside, SMEM), (recv, VMEM), (owned, VMEM), (one, VMEM), (two, VMEM)],
            [
                ((rows, TILE), f32, VMEM),
                ((2 * RIM, TILE), f32, VMEM),
                ((2 * RIM, TILE), f32, VMEM),
                ((1, 1), i32, SMEM),
                ((1, 1), i32, SMEM),
                ((3, room, TILE), i32, VMEM),
                ((room,), i32, SMEM),
                ((room,), i32, SMEM),
                ((groups * PAD if back else 8, TILE), f32, VMEM),
            ],
            [
                pltpu.VMEM((rows, TILE), f32),
                pltpu.VMEM((SLOTS, room, TILE), f32),
                pltpu.VMEM((room, TILE), i32),
                pltpu.VMEM((10, room, TILE), f32),
                pltpu.VMEM((rows * 8, TILE), f32),
                pltpu.SMEM((room,), i32),
            ],
        )

    def unpack(slot, back, extra):
        return call(
            unpack_kernel,
            "unpack",
            [(slot, VMEM), (back, VMEM), (extra, VMEM)],
            [((1, tiles), f32, VMEM)],
        )[0]

    def later_rounds(rounds, state, work):
        def body(now):
            return (now[0] + 1, work(pack(now[0].reshape(1, 1)), now[1]))

        return lax.while_loop(lambda now: now[0] < rounds[0, 0], body, (jnp.int32(1), state))[1]

    low, high = owned[:RIM], owned[own_rows - RIM :]
    rims = swap(jnp.where(odd, high, low), jnp.where(odd, low, high))
    send, slot = pack(jnp.zeros((1, 1), i32))
    recv = exchange(send)
    first = ascend(recv, rims[0], owned, rims[1], False)
    rounds, total, words, base_of, slot_of = first[3:8]

    def more_ascent(packed, state):
        found = ascend(exchange(packed[0]), rims[0], owned, rims[1], False)
        return tuple(now + term for now, term in zip(state, found[:3]))

    grad, one, two = later_rounds(rounds, tuple(first[:3]), more_ascent)
    edges = swap(one, two)

    def last_round(packed, state):
        filler = jnp.zeros((rows - 4 * RIM, TILE), f32)
        below, above = sides(*rims)
        under, over = sides(*edges)
        atlas = jnp.concatenate([below, owned, above]) + ascent * (
            grad + jnp.concatenate([under, filler, over])
        )
        low = atlas[:RIM] * inside[0, 0]
        high = atlas[RIM + own_rows :] * inside[0, 1]
        one, two = sides(low, high)
        found = ascend(exchange(packed[0]), one, atlas[RIM : RIM + own_rows], two, True)
        return state[0] + found[0], unpack(packed[1], exchange(found[8]), state[1])

    extra, extra_correl = later_rounds(
        rounds, (jnp.zeros((rows, TILE), f32), jnp.zeros((1, tiles), f32)), last_round
    )
    atlas, slope, correl_rows = call(
        forward_kernel,
        "forward",
        [
            (total, SMEM), (base_of, SMEM), (slot_of, SMEM), (inside, SMEM), (words, VMEM),
            (owned, VMEM), (rims[0], VMEM), (rims[1], VMEM), (grad, VMEM), (edges[0], VMEM), (edges[1], VMEM),
        ],
        [((own_rows, TILE), f32, VMEM), ((room, TILE), f32, VMEM), ((groups * PAD, TILE), f32, VMEM)],
        [pltpu.VMEM((rows, TILE), f32), pltpu.VMEM((SLOTS, room, TILE), f32), pltpu.VMEM((room, TILE), f32)],
    )
    back = exchange(correl_rows)
    near, one, two = call(
        backward_kernel,
        "backward",
        [(total, SMEM), (base_of, SMEM), (inside, SMEM), (words, VMEM), (slope, VMEM), (atlas, VMEM), (extra, VMEM)],
        [((own_rows, TILE), f32, VMEM), ((RIM, TILE), f32, VMEM), ((RIM, TILE), f32, VMEM)],
        [pltpu.VMEM((room, TILE), i32), pltpu.VMEM((9, room, TILE), f32), pltpu.VMEM((rows * 8, TILE), f32)],
        30_000_000,
    )
    last = swap(one, two)
    current, correl = call(
        finish_kernel,
        "finish",
        [(inside, SMEM), (near, VMEM), (last[0], VMEM), (last[1], VMEM), (slot, VMEM), (back, VMEM), (extra_correl, VMEM)],
        [((own_rows, TILE), f32, VMEM), ((1, tiles), f32, VMEM)],
        (),
        100_000,
    )
    return (current[None], correl[None])


def solution(mesh):
    in_specs = (
        P("slab", "subj", None),
        P("subj", "slab", None, None),
        P("subj", "slab", None, None),
        P("subj", "slab", None, None, None),
        P("subj", "slab", None, None, None),
        P("subj", "slab"),
    )
    out_specs = (P("slab", "subj", None), P("subj", "slab", None))
    return jax.shard_map(shards, mesh=mesh, in_specs=in_specs, out_specs=out_specs, check_vma=False)
```

profile of v0, /device:TPU:64, one launch (start us, length us, event | category | flops | bytes accessed | tf_op | source)
XLA Modules:
  0.0 66.7 jit_solution(8033241237202126739)
XLA Ops:
  1.3 0.0 copy-start.3
  1.3 0.7 %copy-done.3 = s32[1,1,4,256]{3,2,1,0:T(4,128)S(1)} copy-done((s32[1,1,4,256]{3,2,1,0:T(4,128)S(1)}, s32[1,1,4,256]{3,2,1,0:T(4,128)}, u32[]{:S(2)}) %copy-start.3) | copy-done | bytes 4120
  2.0 3.4 %pack.3 = (s32[1792,128]{1,0:T(8,128)}, s32[1,256]{1,0:T(1,128)S(1)}) custom-call(s32[1,1]{1,0:T(1,128)S(6)} %copy.45.refs_0_, s32[1,1]{1,0:T(1,128)} %constant.39.clone.1.refs_1_, s32[4,256]{1,0:T(4,128)S(1)} %bitcast.100, s32[256,8,128]{2,1,0:T(8,128)} %bitcast.24.refs_3_, f32[3,256,128]{2,1,0:T(8,128)} %bitcast.93, bf16[256,128]{1,0:T(8,128)(2,1)} %bitcast.97), custom_call_target="tpu_custom_call" | custom-call | bytes 3000000 | tf_op jit(solution)/shard_map/pack/pallas_call | solution.py:413
  5.4 0.0 copy-start.1
  5.4 5.8 %all-to-all-start.3 = ((s32[16,112,128]{2,1,0:T(8,128)}), s32[16,112,128]{2,1,0:T(8,128)S(1)}, u32[]{:S(2)}, u32[]{:S(2)}) async-start(s32[16,112,128]{2,1,0:T(8,128)} %bitcast.28), calls=%async_computation.3 | async-start | bytes 1835008 | tf_op jit(solution)/shard_map/all_to_all | solution.py:453
  11.2 0.0 copy-done.1
  11.2 0.5 collective-permute-start.1
  11.7 6.3 %collective-permute-start = (f32[8,128]{1,0:T(8,128)S(1)}, f32[8,128]{1,0:T(8,128)S(1)}, u32[]{:S(2)}, u32[]{:S(2)}) collective-permute-start(f32[8,128]{1,0:T(8,128)S(1)} %get-tuple-element.286), channel_id=1, source_target_pairs={{8,16},{24,32},{40,48},{56,64},{72,80},{88,96},{104,112},{120,1},{... | collective-permute-start | bytes 12296 | tf_op jit(solution)/shard_map/ppermute | solution.py:436
  18.0 0.1 add_convert_fusion.refs_1_.inside_ref
  18.1 8.2 %all-to-all-done.3 = s32[16,112,128]{2,1,0:T(8,128)S(1)} async-done(((s32[16,112,128]{2,1,0:T(8,128)}), s32[16,112,128]{2,1,0:T(8,128)S(1)}, u32[]{:S(2)}, u32[]{:S(2)}) %all-to-all-start.3) | async-done | bytes 917536 | tf_op jit(solution)/shard_map/all_to_all | solution.py:453
  26.3 0.0 collective-permute-done.1.refs_5_.second_ref
  26.3 0.0 collective-permute-done.refs_4_.first_ref
  26.3 0.0 copy-start
  26.3 0.0 copy-start.2
  26.3 7.5 %ascend.3 = (f32[272,128]{1,0:T(8,128)S(1)}, f32[16,128]{1,0:T(8,128)S(1)}, f32[16,128]{1,0:T(8,128)S(1)}, s32[1,1]{1,0:T(1,128)}, s32[1,1]{1,0:T(1,128)}, /*ind...) custom-call(s32[16,128]{1,0:T(8,128)S(1)} %bitcast.92, ...), custom_call_target="tpu_custom_call" | custom-call | bytes 3000000 | tf_op jit(solution)/shard_map/ascend/pallas_call | solution.py:413
  33.8 0.0 copy-done
  33.8 0.0 copy-done.2
  33.9 0.7 %while.26 = (s32[]{:T(128)}, f32[272,128]{1,0:T(8,128)S(1)}, f32[16,128]{1,0:T(8,128)S(1)}, f32[16,128]{1,0:T(8,128)S(1)}, s32[1,1]{1,0:T(1,128)}, /*index=5*/s3...) while((s32[]{:T(128)}, f32[272,128]{1,0:T(8,128)S(1)}, ...), condition=%wide.region_1.2_spmd, body=%wide.region_0.1_spmd.sunk | while | flops 38914 | bytes 9236013 | solution.py:498
  34.5 0.1 collective-permute-start.3
  34.6 1.9 %collective-permute-start.2 = (f32[16,128]{1,0:T(8,128)S(1)}, f32[16,128]{1,0:T(8,128)S(1)}, u32[]{:S(2)}, u32[]{:S(2)}) collective-permute-start(f32[16,128]{1,0:T(8,128)S(1)} %get-tuple-element.202), channel_id=1, source_target_pairs={{8,16},{24,32},{40,48},{56,64},{72,80},{88,96},{104,112},{120,1},{... | collective-permute-start | bytes 24584 | tf_op jit(solution)/shard_map/ppermute | solution.py:436
  36.6 0.0 collective-permute-done.3.two_ref
  36.6 7.2 %collective-permute-done.2.one_ref = f32[16,128]{1,0:T(8,128)S(1)} collective-permute-done((f32[16,128]{1,0:T(8,128)S(1)}, f32[16,128]{1,0:T(8,128)S(1)}, u32[]{:S(2)}, u32[]{:S(2)}) %collective-permute-start.2) | collective-permute-done | bytes 8224 | tf_op jit(solution)/shard_map/ppermute | solution.py:436
  43.8 4.6 %forward.1 = (f32[256,128]{1,0:T(8,128)S(1)}, f32[640,128]{1,0:T(8,128)S(1)}, f32[640,128]{1,0:T(8,128)}) custom-call(s32[1,1]{1,0:T(1,128)} %get-tuple-element.193.total_ref, s32[640]{0:T(1024)S(1)} %get-tuple-element.194.base_of, s32[640]{0:T(1024)S(1)} %get-tuple-element.196.slot_of, f32[1,3]{1,0:T(1,128)S(1)} %get-tuple-element.631, ...), custom_call_target="tpu_custom_call" | custom-call | bytes 3000000 | tf_op jit(solution)/shard_map/forward/pallas_call | solution.py:413
  48.4 0.7 %while.27 = (s32[]{:T(128)}, f32[272,128]{1,0:T(8,128)S(1)}, f32[1,256]{1,0:T(1,128)S(1)}, s32[1,1]{1,0:T(1,128)}, s32[1,1,4,256]{3,2,1,0:T(4,128)S(1)}, /*index...) while((s32[]{:T(128)}, f32[272,128]{1,0:T(8,128)S(1)}, ...), condition=%wide.region_3.4_spmd, body=%wide.region_2.3_spmd.sunk | while | flops 288770 | bytes 13938008 | solution.py:498
  49.1 3.6 %all-to-all-start.4 = ((f32[16,40,128]{2,1,0:T(8,128)}), f32[16,40,128]{2,1,0:T(8,128)S(1)}, u32[]{:S(2)}, u32[]{:S(2)}) async-start(f32[16,40,128]{2,1,0:T(8,128)} %bitcast.35), calls=%async_computation.4 | async-start | bytes 655360 | tf_op jit(solution)/shard_map/all_to_all | solution.py:453
  52.7 3.6 %backward.1 = (f32[256,128]{1,0:T(8,128)S(1)}, f32[8,128]{1,0:T(8,128)S(1)}, f32[8,128]{1,0:T(8,128)S(1)}) custom-call(s32[1,1]{1,0:T(1,128)} %get-tuple-element.193.total_ref, s32[640]{0:T(1024)S(1)} %get-tuple-element.194.base_of, f32[1,3]{1,0:T(1,128)S(1)} %get-tuple-element.632, s32[3,640,128]{2,1,0:T(8,128)S(1)} %get-tuple-element.195.words, ...), custom_call_target="tpu_custom_call" | custom-call | bytes 30000000 | tf_op jit(solution)/shard_map/backward/pallas_call | solution.py:413
  56.3 4.8 %collective-permute-start.4 = (f32[8,128]{1,0:T(8,128)S(1)}, f32[8,128]{1,0:T(8,128)S(1)}, u32[]{:S(2)}, u32[]{:S(2)}) collective-permute-start(f32[8,128]{1,0:T(8,128)S(1)} %get-tuple-element.208), channel_id=1, source_target_pairs={{8,16},{24,32},{40,48},{56,64},{72,80},{88,96},{104,112},{120,1},{... | collective-permute-start | bytes 12296 | tf_op jit(solution)/shard_map/ppermute | solution.py:436
  61.2 0.1 collective-permute-start.5
  61.3 4.2 %collective-permute-done.4.one_ref = f32[8,128]{1,0:T(8,128)S(1)} collective-permute-done((f32[8,128]{1,0:T(8,128)S(1)}, f32[8,128]{1,0:T(8,128)S(1)}, u32[]{:S(2)}, u32[]{:S(2)}) %collective-permute-start.4) | collective-permute-done | bytes 4128 | tf_op jit(solution)/shard_map/ppermute | solution.py:436
  65.5 0.0 collective-permute-done.5.two_ref
  65.5 0.0 all-to-all-done.4
  65.5 1.2 %finish.1 = (f32[256,128]{1,0:T(8,128)}, f32[1,256]{1,0:T(1,128)}) custom-call(f32[1,3]{1,0:T(1,128)S(1)} %get-tuple-element.632, f32[256,128]{1,0:T(8,128)S(1)} %get-tuple-element.207.near_ref, f32[8,128]{1,0:T(8,128)S(1)} %collective-permute-done.4.one_ref, f32[8,128]{1,0:T(8,128)S(1)} %collective-permute-done.5.two_ref, ...), custom_call_target="tpu_custom_call" | custom-call | bytes 100000 | tf_op jit(solution)/shard_map/finish/pallas_call | solution.py:413
  (4 shorter events, 0.0 us)
Async XLA Ops:
  1.3 0.7 %copy-start.3 = (s32[1,1,4,256]{3,2,1,0:T(4,128)S(1)}, s32[1,1,4,256]{3,2,1,0:T(4,128)}, u32[]{:S(2)}) copy-start(s32[1,1,4,256]{3,2,1,0:T(4,128)} %param.12) | copy-start | bytes 12292
  5.4 5.8 %copy-start.1 = (f32[1,256,128]{2,1,0:T(8,128)S(1)}, f32[1,256,128]{2,1,0:T(8,128)}, u32[]{:S(2)}) copy-start(f32[1,256,128]{2,1,0:T(8,128)} %param.10) | copy-start | bytes 393220
  5.4 20.8 %all-to-all-start.3 = ((s32[16,112,128]{2,1,0:T(8,128)}), s32[16,112,128]{2,1,0:T(8,128)S(1)}, u32[]{:S(2)}, u32[]{:S(2)}) async-start(s32[16,112,128]{2,1,0:T(8,128)} %bitcast.28), calls=%async_computation.3 | async-start | bytes 1835008 | tf_op jit(solution)/shard_map/all_to_all | solution.py:453
  11.2 15.1 %collective-permute-start.1 = (f32[8,128]{1,0:T(8,128)S(1)}, f32[8,128]{1,0:T(8,128)S(1)}, u32[]{:S(2)}, u32[]{:S(2)}) collective-permute-start(f32[8,128]{1,0:T(8,128)S(1)} %get-tuple-element.285), channel_id=1, source_target_pairs={{0,8},{16,24},{32,40},{48,56},{64,72},{80,88},{96,104},{112,120},{... | collective-permute-start | bytes 12296 | tf_op jit(solution)/shard_map/ppermute | solution.py:436
  11.7 14.6 %collective-permute-start = (f32[8,128]{1,0:T(8,128)S(1)}, f32[8,128]{1,0:T(8,128)S(1)}, u32[]{:S(2)}, u32[]{:S(2)}) collective-permute-start(f32[8,128]{1,0:T(8,128)S(1)} %get-tuple-element.286), channel_id=1, source_target_pairs={{8,16},{24,32},{40,48},{56,64},{72,80},{88,96},{104,112},{120,1},{... | collective-permute-start | bytes 12296 | tf_op jit(solution)/shard_map/ppermute | solution.py:436
  26.3 7.6 %copy-start = (f32[1,1,256,3,128]{4,2,3,1,0:T(8,128)S(1)}, f32[1,1,256,3,128]{4,2,3,1,0:T(8,128)}, u32[]{:S(2)}) copy-start(f32[1,1,256,3,128]{4,2,3,1,0:T(8,128)} %param.14) | copy-start | bytes 1179652
  26.3 7.6 %copy-start.2 = (bf16[1,1,256,128]{3,2,1,0:T(8,128)(2,1)S(1)}, bf16[1,1,256,128]{3,2,1,0:T(8,128)(2,1)}, u32[]{:S(2)}) copy-start(bf16[1,1,256,128]{3,2,1,0:T(8,128)(2,1)} %param.11) | copy-start | bytes 196612
  34.5 2.0 %collective-permute-start.3 = (f32[16,128]{1,0:T(8,128)S(1)}, f32[16,128]{1,0:T(8,128)S(1)}, u32[]{:S(2)}, u32[]{:S(2)}) collective-permute-start(f32[16,128]{1,0:T(8,128)S(1)} %get-tuple-element.203), channel_id=1, source_target_pairs={{0,8},{16,24},{32,40},{48,56},{64,72},{80,88},{96,104},{112,120},{... | collective-permute-start | bytes 24584 | tf_op jit(solution)/shard_map/ppermute | solution.py:436
  34.6 9.2 %collective-permute-start.2 = (f32[16,128]{1,0:T(8,128)S(1)}, f32[16,128]{1,0:T(8,128)S(1)}, u32[]{:S(2)}, u32[]{:S(2)}) collective-permute-start(f32[16,128]{1,0:T(8,128)S(1)} %get-tuple-element.202), channel_id=1, source_target_pairs={{8,16},{24,32},{40,48},{56,64},{72,80},{88,96},{104,112},{120,1},{... | collective-permute-start | bytes 24584 | tf_op jit(solution)/shard_map/ppermute | solution.py:436
  49.1 16.3 %all-to-all-start.4 = ((f32[16,40,128]{2,1,0:T(8,128)}), f32[16,40,128]{2,1,0:T(8,128)S(1)}, u32[]{:S(2)}, u32[]{:S(2)}) async-start(f32[16,40,128]{2,1,0:T(8,128)} %bitcast.35), calls=%async_computation.4 | async-start | bytes 655360 | tf_op jit(solution)/shard_map/all_to_all | solution.py:453
  56.3 9.1 %collective-permute-start.4 = (f32[8,128]{1,0:T(8,128)S(1)}, f32[8,128]{1,0:T(8,128)S(1)}, u32[]{:S(2)}, u32[]{:S(2)}) collective-permute-start(f32[8,128]{1,0:T(8,128)S(1)} %get-tuple-element.208), channel_id=1, source_target_pairs={{8,16},{24,32},{40,48},{56,64},{72,80},{88,96},{104,112},{120,1},{... | collective-permute-start | bytes 12296 | tf_op jit(solution)/shard_map/ppermute | solution.py:436
  61.2 4.3 %collective-permute-start.5 = (f32[8,128]{1,0:T(8,128)S(1)}, f32[8,128]{1,0:T(8,128)S(1)}, u32[]{:S(2)}, u32[]{:S(2)}) collective-permute-start(f32[8,128]{1,0:T(8,128)S(1)} %get-tuple-element.209), channel_id=1, source_target_pairs={{0,8},{16,24},{32,40},{48,56},{64,72},{80,88},{96,104},{112,120},{... | collective-permute-start | bytes 12296 | tf_op jit(solution)/shard_map/ppermute | solution.py:436
where the time goes:
time: 67.2 us; the launch traced here: 66.7 us
  starting transfers between devices  23 us (34%)
  Pallas kernels  20.4 us (30%)
  waiting for transfers between devices  19.6 us (29%)
  between operations  1.47 us (2%)
  loops' own time  1.37 us (2%)
  local copies, waits for them, and re-layouts  0.72 us (1%)
    pallas_call x5, Pallas kernels, call(): pl.pallas_call(kernel, out_shape=[jax.ShapeDtypeStruct(shape, kind) for s...  20.4 us
    ppermute x3, starting transfers between devices, swap(): lax.ppermute(one, both, pairs_from(1))  13.1 us
    ppermute x3, waiting for transfers between devices, swap(): lax.ppermute(one, both, pairs_from(1))  11.5 us
    all_to_all x2, starting transfers between devices, exchange(): return lax.all_to_all(send, 'subj', 0, 0, tiled=True)  9.32 us
    all_to_all x2, waiting for transfers between devices, exchange(): return lax.all_to_all(send, 'subj', 0, 0, tiled=True)  8.15 us
    another operation x2, loops' own time, later_rounds(): lax.while_loop(lambda now: now[0] < rounds[0, 0], body, (jnp.int32(1), st...  1.37 us
  transfers between devices with their start and end apart: 8, of which 3 were waited for; matrix products, arithmetic and copies ran while one was open for 0% of the time, Pallas kernels for 5%

commit v1 on v0

--- a/solution.py
+++ b/solution.py
@@ -491,11 +491,11 @@
             [((1, tiles), f32, VMEM)],
         )[0]
 
-    def later_rounds(rounds, state, work):
+    def later_rounds(later, state, work):
         def body(now):
-            return (now[0] + 1, work(pack(now[0].reshape(1, 1)), now[1]))
-
-        return lax.while_loop(lambda now: now[0] < rounds[0, 0], body, (jnp.int32(1), state))[1]
+            return (now[0] - 1, work(pack(now[0].reshape(1, 1)), now[1]))
+
+        return lax.while_loop(lambda now: now[0] > 0, body, (later, state))[1]
 
     low, high = owned[:RIM], owned[own_rows - RIM :]
     rims = swap(jnp.where(odd, high, low), jnp.where(odd, low, high))
@@ -503,12 +503,13 @@
     recv = exchange(send)
     first = ascend(recv, rims[0], owned, rims[1], False)
     rounds, total, words, base_of, slot_of = first[3:8]
+    later = rounds[0, 0] - 1
 
     def more_ascent(packed, state):
         found = ascend(exchange(packed[0]), rims[0], owned, rims[1], False)
         return tuple(now + term for now, term in zip(state, found[:3]))
 
-    grad, one, two = later_rounds(rounds, tuple(first[:3]), more_ascent)
+    grad, one, two = later_rounds(later, tuple(first[:3]), more_ascent)
     edges = swap(one, two)
 
     def last_round(packed, state):
@@ -525,7 +526,7 @@
         return state[0] + found[0], unpack(packed[1], exchange(found[8]), state[1])
 
     extra, extra_correl = later_rounds(
-        rounds, (jnp.zeros((rows, TILE), f32), jnp.zeros((1, tiles), f32)), last_round
+        later, (jnp.zeros((rows, TILE), f32), jnp.zeros((1, tiles), f32)), last_round
     )
     atlas, slope, correl_rows = call(
         forward_kernel,

time: 67.2 us -> 66.7 us (level)
  starting transfers between devices: 23 us -> 24.6 us
  waiting for transfers between devices: 19.6 us -> 18 us
  loops' own time: 1.37 us -> 0.02 us
    ppermute x3, starting transfers between devices: 13.1 us -> 14.7 us  [swap(): lax.ppermute(one, both, pairs_from(1))]
    ppermute x3, waiting for transfers between devices: 11.5 us -> 9.86 us  [swap(): lax.ppermute(one, both, pairs_from(1))]
    another operation x2, loops' own time: 1.37 us -> 0.02 us  [later_rounds(): return lax.while_loop(lambda now: now[0] > 0, body, (later, state))[1]]
  transfers between devices with their start and end apart: 8 -> 8, of which waited for: 3 -> 3; matrix products, arithmetic and copies ran while one was open for 0% -> 0% of each run, Pallas kernels for 5% -> 6%
where the time goes in v1:
time: 66.7 us; the launch traced here: 66.2 us
  starting transfers between devices  24.6 us (37%)
  Pallas kernels  20.6 us (31%)
  waiting for transfers between devices  18 us (27%)
  between operations  2.12 us (3%)
  local copies, waits for them, and re-layouts  0.72 us (1%)
    pallas_call x5, Pallas kernels, call(): pl.pallas_call(kernel, out_shape=[jax.ShapeDtypeStruct(shape, kind) for s...  20.6 us
    ppermute x3, starting transfers between devices, swap(): lax.ppermute(one, both, pairs_from(1))  14.7 us
    ppermute x3, waiting for transfers between devices, swap(): lax.ppermute(one, both, pairs_from(1))  9.86 us
    all_to_all x2, starting transfers between devices, exchange(): return lax.all_to_all(send, 'subj', 0, 0, tiled=True)  9.32 us
    all_to_all x2, waiting for transfers between devices, exchange(): return lax.all_to_all(send, 'subj', 0, 0, tiled=True)  8.15 us
  transfers between devices with their start and end apart: 8, of which 3 were waited for; matrix products, arithmetic and copies ran while one was open for 0% of the time, Pallas kernels for 6%

profile of v1, /device:TPU:64, one launch (start us, length us, event | category | flops | bytes accessed | tf_op | source)
XLA Modules:
  0.0 66.2 jit_solution(9882079022642611599)
XLA Ops:
  1.3 0.0 copy-start.3
  1.3 0.7 %copy-done.3 = s32[1,1,4,256]{3,2,1,0:T(4,128)S(1)} copy-done((s32[1,1,4,256]{3,2,1,0:T(4,128)S(1)}, s32[1,1,4,256]{3,2,1,0:T(4,128)}, u32[]{:S(2)}) %copy-start.3) | copy-done | bytes 4120
  2.0 3.4 %pack.9 = (s32[1792,128]{1,0:T(8,128)}, s32[1,256]{1,0:T(1,128)S(1)}) custom-call(s32[1,1]{1,0:T(1,128)S(6)} %copy.45.refs_0_, s32[1,1]{1,0:T(1,128)} %constant.63.clone.1.refs_1_, s32[4,256]{1,0:T(4,128)S(1)} %bitcast.97, s32[256,8,128]{2,1,0:T(8,128)} %bitcast.22.refs_3_, f32[3,256,128]{2,1,0:T(8,128)} %bitcast.90, bf16[256,128]{1,0:T(8,128)(2,1)} %bitcast.94), custom_call_target="tpu_custom_call" | custom-call | bytes 3000000 | tf_op jit(solution)/shard_map/pack/pallas_call | solution.py:413
  5.4 0.0 copy-start.1
  5.4 5.8 %all-to-all-start.3 = ((s32[16,112,128]{2,1,0:T(8,128)}), s32[16,112,128]{2,1,0:T(8,128)S(1)}, u32[]{:S(2)}, u32[]{:S(2)}) async-start(s32[16,112,128]{2,1,0:T(8,128)} %bitcast.26), calls=%async_computation.3 | async-start | bytes 1835008 | tf_op jit(solution)/shard_map/all_to_all | solution.py:453
  11.2 0.0 copy-done.1
  11.2 0.5 collective-permute-start.1
  11.7 6.3 %collective-permute-start = (f32[8,128]{1,0:T(8,128)S(1)}, f32[8,128]{1,0:T(8,128)S(1)}, u32[]{:S(2)}, u32[]{:S(2)}) collective-permute-start(f32[8,128]{1,0:T(8,128)S(1)} %get-tuple-element.468), channel_id=1, source_target_pairs={{8,16},{24,32},{40,48},{56,64},{72,80},{88,96},{104,112},{120,1},{... | collective-permute-start | bytes 12296 | tf_op jit(solution)/shard_map/ppermute | solution.py:436
  18.0 0.1 add_convert_fusion.refs_1_.inside_ref
  18.1 8.2 %all-to-all-done.3 = s32[16,112,128]{2,1,0:T(8,128)S(1)} async-done(((s32[16,112,128]{2,1,0:T(8,128)}), s32[16,112,128]{2,1,0:T(8,128)S(1)}, u32[]{:S(2)}, u32[]{:S(2)}) %all-to-all-start.3) | async-done | bytes 917536 | tf_op jit(solution)/shard_map/all_to_all | solution.py:453
  26.3 0.0 collective-permute-done.1.refs_5_.second_ref
  26.3 0.0 collective-permute-done.refs_4_.first_ref
  26.3 0.0 copy-start
  26.3 0.0 copy-start.2
  26.3 7.5 %ascend.9 = (f32[272,128]{1,0:T(8,128)S(1)}, f32[16,128]{1,0:T(8,128)S(1)}, f32[16,128]{1,0:T(8,128)S(1)}, s32[1,1]{1,0:T(1,128)}, s32[1,1]{1,0:T(1,128)}, /*ind...) custom-call(s32[16,128]{1,0:T(8,128)S(1)} %bitcast.89, ...), custom_call_target="tpu_custom_call" | custom-call | bytes 3000000 | tf_op jit(solution)/shard_map/ascend/pallas_call | solution.py:413
  34.5 0.0 copy-done
  34.5 0.0 copy-done.2
  34.5 0.1 collective-permute-start.3
  34.6 2.9 %collective-permute-start.2 = (f32[16,128]{1,0:T(8,128)S(1)}, f32[16,128]{1,0:T(8,128)S(1)}, u32[]{:S(2)}, u32[]{:S(2)}) collective-permute-start(f32[16,128]{1,0:T(8,128)S(1)} %get-tuple-element.388), channel_id=1, source_target_pairs={{8,16},{24,32},{40,48},{56,64},{72,80},{88,96},{104,112},{120,1},{... | collective-permute-start | bytes 24584 | tf_op jit(solution)/shard_map/ppermute | solution.py:436
  37.5 0.0 collective-permute-done.3.two_ref
  37.5 6.3 %collective-permute-done.2.one_ref = f32[16,128]{1,0:T(8,128)S(1)} collective-permute-done((f32[16,128]{1,0:T(8,128)S(1)}, f32[16,128]{1,0:T(8,128)S(1)}, u32[]{:S(2)}, u32[]{:S(2)}) %collective-permute-start.2) | collective-permute-done | bytes 8224 | tf_op jit(solution)/shard_map/ppermute | solution.py:436
  43.8 4.7 %forward.1 = (f32[256,128]{1,0:T(8,128)S(1)}, f32[640,128]{1,0:T(8,128)S(1)}, f32[640,128]{1,0:T(8,128)}) custom-call(s32[1,1]{1,0:T(1,128)} %get-tuple-element.379.total_ref, s32[640]{0:T(1024)S(1)} %get-tuple-element.380.base_of, s32[640]{0:T(1024)S(1)} %get-tuple-element.382.slot_of, f32[1,3]{1,0:T(1,128)S(1)} %get-tuple-element.793, ...), custom_call_target="tpu_custom_call" | custom-call | bytes 3000000 | tf_op jit(solution)/shard_map/forward/pallas_call | solution.py:413
  48.5 3.6 %all-to-all-start.4 = ((f32[16,40,128]{2,1,0:T(8,128)}), f32[16,40,128]{2,1,0:T(8,128)S(1)}, u32[]{:S(2)}, u32[]{:S(2)}) async-start(f32[16,40,128]{2,1,0:T(8,128)} %bitcast.34), calls=%async_computation.4 | async-start | bytes 655360 | tf_op jit(solution)/shard_map/all_to_all | solution.py:453
  52.1 3.8 %backward.1 = (f32[256,128]{1,0:T(8,128)S(1)}, f32[8,128]{1,0:T(8,128)S(1)}, f32[8,128]{1,0:T(8,128)S(1)}) custom-call(s32[1,1]{1,0:T(1,128)} %get-tuple-element.379.total_ref, s32[640]{0:T(1024)S(1)} %get-tuple-element.380.base_of, f32[1,3]{1,0:T(1,128)S(1)} %get-tuple-element.794, s32[3,640,128]{2,1,0:T(8,128)S(1)} %get-tuple-element.381.words, ...), custom_call_target="tpu_custom_call" | custom-call | bytes 30000000 | tf_op jit(solution)/shard_map/backward/pallas_call | solution.py:413
  55.8 5.5 %collective-permute-start.4 = (f32[8,128]{1,0:T(8,128)S(1)}, f32[8,128]{1,0:T(8,128)S(1)}, u32[]{:S(2)}, u32[]{:S(2)}) collective-permute-start(f32[8,128]{1,0:T(8,128)S(1)} %get-tuple-element.394), channel_id=1, source_target_pairs={{8,16},{24,32},{40,48},{56,64},{72,80},{88,96},{104,112},{120,1},{... | collective-permute-start | bytes 12296 | tf_op jit(solution)/shard_map/ppermute | solution.py:436
  61.3 0.1 collective-permute-start.5
  61.4 3.6 %collective-permute-done.4.one_ref = f32[8,128]{1,0:T(8,128)S(1)} collective-permute-done((f32[8,128]{1,0:T(8,128)S(1)}, f32[8,128]{1,0:T(8,128)S(1)}, u32[]{:S(2)}, u32[]{:S(2)}) %collective-permute-start.4) | collective-permute-done | bytes 4128 | tf_op jit(solution)/shard_map/ppermute | solution.py:436
  65.0 0.0 collective-permute-done.5.two_ref
  65.0 0.0 all-to-all-done.4
  65.0 1.2 %finish.1 = (f32[256,128]{1,0:T(8,128)}, f32[1,256]{1,0:T(1,128)}) custom-call(f32[1,3]{1,0:T(1,128)S(1)} %get-tuple-element.794, f32[256,128]{1,0:T(8,128)S(1)} %get-tuple-element.393.near_ref, f32[8,128]{1,0:T(8,128)S(1)} %collective-permute-done.4.one_ref, f32[8,128]{1,0:T(8,128)S(1)} %collective-permute-done.5.two_ref, ...), custom_call_target="tpu_custom_call" | custom-call | bytes 100000 | tf_op jit(solution)/shard_map/finish/pallas_call | solution.py:413
  (6 shorter events, 0.0 us)
Async XLA Ops:
  1.3 0.7 %copy-start.3 = (s32[1,1,4,256]{3,2,1,0:T(4,128)S(1)}, s32[1,1,4,256]{3,2,1,0:T(4,128)}, u32[]{:S(2)}) copy-start(s32[1,1,4,256]{3,2,1,0:T(4,128)} %param.12) | copy-start | bytes 12292
  5.4 5.8 %copy-start.1 = (f32[1,256,128]{2,1,0:T(8,128)S(1)}, f32[1,256,128]{2,1,0:T(8,128)}, u32[]{:S(2)}) copy-start(f32[1,256,128]{2,1,0:T(8,128)} %param.10) | copy-start | bytes 393220
  5.4 20.8 %all-to-all-start.3 = ((s32[16,112,128]{2,1,0:T(8,128)}), s32[16,112,128]{2,1,0:T(8,128)S(1)}, u32[]{:S(2)}, u32[]{:S(2)}) async-start(s32[16,112,128]{2,1,0:T(8,128)} %bitcast.26), calls=%async_computation.3 | async-start | bytes 1835008 | tf_op jit(solution)/shard_map/all_to_all | solution.py:453
  11.2 15.1 %collective-permute-start.1 = (f32[8,128]{1,0:T(8,128)S(1)}, f32[8,128]{1,0:T(8,128)S(1)}, u32[]{:S(2)}, u32[]{:S(2)}) collective-permute-start(f32[8,128]{1,0:T(8,128)S(1)} %get-tuple-element.467), channel_id=1, source_target_pairs={{0,8},{16,24},{32,40},{48,56},{64,72},{80,88},{96,104},{112,120},{... | collective-permute-start | bytes 12296 | tf_op jit(solution)/shard_map/ppermute | solution.py:436
  11.7 14.6 %collective-permute-start = (f32[8,128]{1,0:T(8,128)S(1)}, f32[8,128]{1,0:T(8,128)S(1)}, u32[]{:S(2)}, u32[]{:S(2)}) collective-permute-start(f32[8,128]{1,0:T(8,128)S(1)} %get-tuple-element.468), channel_id=1, source_target_pairs={{8,16},{24,32},{40,48},{56,64},{72,80},{88,96},{104,112},{120,1},{... | collective-permute-start | bytes 12296 | tf_op jit(solution)/shard_map/ppermute | solution.py:436
  26.3 8.2 %copy-start = (f32[1,1,256,3,128]{4,2,3,1,0:T(8,128)S(1)}, f32[1,1,256,3,128]{4,2,3,1,0:T(8,128)}, u32[]{:S(2)}) copy-start(f32[1,1,256,3,128]{4,2,3,1,0:T(8,128)} %param.14) | copy-start | bytes 1179652
  26.3 8.2 %copy-start.2 = (bf16[1,1,256,128]{3,2,1,0:T(8,128)(2,1)S(1)}, bf16[1,1,256,128]{3,2,1,0:T(8,128)(2,1)}, u32[]{:S(2)}) copy-start(bf16[1,1,256,128]{3,2,1,0:T(8,128)(2,1)} %param.11) | copy-start | bytes 196612
  34.5 3.0 %collective-permute-start.3 = (f32[16,128]{1,0:T(8,128)S(1)}, f32[16,128]{1,0:T(8,128)S(1)}, u32[]{:S(2)}, u32[]{:S(2)}) collective-permute-start(f32[16,128]{1,0:T(8,128)S(1)} %get-tuple-element.389), channel_id=1, source_target_pairs={{0,8},{16,24},{32,40},{48,56},{64,72},{80,88},{96,104},{112,120},{... | collective-permute-start | bytes 24584 | tf_op jit(solution)/shard_map/ppermute | solution.py:436
  34.6 9.2 %collective-permute-start.2 = (f32[16,128]{1,0:T(8,128)S(1)}, f32[16,128]{1,0:T(8,128)S(1)}, u32[]{:S(2)}, u32[]{:S(2)}) collective-permute-start(f32[16,128]{1,0:T(8,128)S(1)} %get-tuple-element.388), channel_id=1, source_target_pairs={{8,16},{24,32},{40,48},{56,64},{72,80},{88,96},{104,112},{120,1},{... | collective-permute-start | bytes 24584 | tf_op jit(solution)/shard_map/ppermute | solution.py:436
  48.5 16.5 %all-to-all-start.4 = ((f32[16,40,128]{2,1,0:T(8,128)}), f32[16,40,128]{2,1,0:T(8,128)S(1)}, u32[]{:S(2)}, u32[]{:S(2)}) async-start(f32[16,40,128]{2,1,0:T(8,128)} %bitcast.34), calls=%async_computation.4 | async-start | bytes 655360 | tf_op jit(solution)/shard_map/all_to_all | solution.py:453
  55.8 9.1 %collective-permute-start.4 = (f32[8,128]{1,0:T(8,128)S(1)}, f32[8,128]{1,0:T(8,128)S(1)}, u32[]{:S(2)}, u32[]{:S(2)}) collective-permute-start(f32[8,128]{1,0:T(8,128)S(1)} %get-tuple-element.394), channel_id=1, source_target_pairs={{8,16},{24,32},{40,48},{56,64},{72,80},{88,96},{104,112},{120,1},{... | collective-permute-start | bytes 12296 | tf_op jit(solution)/shard_map/ppermute | solution.py:436
  61.3 3.6 %collective-permute-start.5 = (f32[8,128]{1,0:T(8,128)S(1)}, f32[8,128]{1,0:T(8,128)S(1)}, u32[]{:S(2)}, u32[]{:S(2)}) collective-permute-start(f32[8,128]{1,0:T(8,128)S(1)} %get-tuple-element.395), channel_id=1, source_target_pairs={{0,8},{16,24},{32,40},{48,56},{64,72},{80,88},{96,104},{112,120},{... | collective-permute-start | bytes 12296 | tf_op jit(solution)/shard_map/ppermute | solution.py:436
